TPU v7x, 1024 devices: a whole 4x8x16 slice. The times are simulated.
1024 devices in a mesh: grp: 4 (over x), dp: 256 (over z, y, core).
Axes of the slice: x: 4, y: 8, z: 16, core: 2. Of those that a mesh axis runs over, the one named last changes fastest.
Arguments:
- crops_in: bfloat16 [16384, 3, 3, 3072], P(('grp', 'dp')), may hold values from -48 to 48, as said below
- cotangent: bfloat16 [16384, 3, 3, 3072], P(('grp', 'dp')), may hold values from -0.0260416667 to 0.0260416667, as said below
- kernel: float32 [49, 3072], replicated, may hold values from -0.875 to 0.875
- conv_bias: float32 [3072], replicated, may hold values from -3 to 3
- norm_gain: float32 [3072], replicated, may hold values from 0.5 to 1.5
Outputs:
- combined: float32 [52, 3072], P('grp', 'dp')
Inputs may be any that keep to these rules, and one draw needn't show every extreme that they name: `crops_in`: each channel has a mean over all cells; channel scales differ. `cotangent`: each channel has a mean over all cells.
All inputs are finite; a program needn't handle non-finite values.
Results may differ from a plain program's by a relative error of at most 0.00055.
Values sent between devices are 32-bit elements; how exact they have to be, the bound alone decides.
A program may use at most 32 MiB of HBM per device.

v0:
```python
import jax
import jax.numpy as jnp
from jax import lax
from jax.sharding import PartitionSpec as P

KS = 7
GRID = 3
TAPS = 49


def from_partner(value, axis, apart):
    return lax.ppermute(value, axis, [(i, i ^ 1 << apart) for i in range(lax.axis_size(axis))])


def shifted(values, row_off, col_off):
    padded = jnp.pad(values, ((0, 0), (GRID - 1, GRID - 1), (GRID - 1, GRID - 1), (0, 0)))
    return padded[
        :,
        GRID - 1 + row_off : 2 * GRID - 1 + row_off,
        GRID - 1 + col_off : 2 * GRID - 1 + col_off,
        :,
    ]


def block_bucket(crops_in, cotangent, kernel, conv_bias, norm_gain):
    inputs = crops_in.astype(jnp.float32)
    upstream = cotangent.astype(jnp.float32)
    half_side = KS // 2
    conv_out = jnp.zeros_like(inputs) + conv_bias
    for row_tap in range(KS):
        for col_tap in range(KS):
            row_off = row_tap - half_side
            col_off = col_tap - half_side
            if abs(row_off) < GRID and abs(col_off) < GRID:
                conv_out = conv_out + kernel[row_tap * KS + col_tap] * shifted(
                    inputs, row_off, col_off
                )
    centre = jnp.mean(conv_out, -1, keepdims=True)
    spread = jnp.mean(jnp.square(conv_out - centre), -1, keepdims=True)
    scale_inv = lax.rsqrt(spread + 1e-06)
    normed = (conv_out - centre) * scale_inv
    grad_gain = jnp.sum(upstream * normed, (0, 1, 2))
    grad_shift = jnp.sum(upstream, (0, 1, 2))
    scaled = upstream * norm_gain
    grad_conv = scale_inv * (
        scaled
        - jnp.mean(scaled, -1, keepdims=True)
        - normed * jnp.mean(scaled * normed, -1, keepdims=True)
    )
    tap_rows = []
    for row_tap in range(KS):
        for col_tap in range(KS):
            row_off = row_tap - half_side
            col_off = col_tap - half_side
            if abs(row_off) < GRID and abs(col_off) < GRID:
                tap_rows.append(jnp.sum(grad_conv * shifted(inputs, row_off, col_off), (0, 1, 2)))
            else:
                tap_rows.append(jnp.zeros_like(grad_shift))
    grad_bias = jnp.sum(grad_conv, (0, 1, 2))
    return jnp.concatenate(
        [jnp.stack(tap_rows), grad_bias[None], grad_gain[None], grad_shift[None]], 0
    )


def layer_split(values):
    return jnp.concatenate([jnp.sum(values[..., :TAPS], -1, keepdims=True), values[..., TAPS:]], -1)


def expand(coeffs):
    return jnp.concatenate([jnp.broadcast_to(coeffs[:1], (TAPS,)), coeffs[1:]])[:, None]


def blend(lower_vec, upper_vec, layer_sums):
    inner = layer_sums[0]
    norm_low = layer_sums[1]
    norm_high = layer_sums[2]
    return (
        expand(1.0 - inner / (2.0 * norm_low)) * lower_vec
        + expand(1.0 - inner / (2.0 * norm_high)) * upper_vec
    )


def combine_groups(own_shard):
    group_count = lax.axis_size("grp")
    current = own_shard
    for level_bit in range(group_count.bit_length() - 1):
        partner_shard = from_partner(current, "grp", level_bit)
        is_upper = lax.axis_index("grp") // 2**level_bit % 2 == 1
        lower_vec = jnp.where(is_upper, partner_shard, current)
        upper_vec = jnp.where(is_upper, current, partner_shard)
        layer_sums = jnp.stack(
            [
                layer_split(jnp.sum(lower_vec * upper_vec, 1)),
                layer_split(jnp.sum(lower_vec * lower_vec, 1)),
                layer_split(jnp.sum(upper_vec * upper_vec, 1)),
            ]
        )
        layer_sums = lax.psum(layer_sums, "dp")
        current = blend(lower_vec, upper_vec, layer_sums)
    return current


def group_rows(result):
    row_count = result.shape[0] // lax.axis_size("grp")
    return lax.dynamic_slice_in_dim(result, lax.axis_index("grp") * row_count, row_count, 0)


def local(crops_in, cotangent, kernel, conv_bias, norm_gain):
    bucket = block_bucket(crops_in, cotangent, kernel, conv_bias, norm_gain)
    own_shard = lax.psum_scatter(bucket, "dp", scatter_dimension=1, tiled=True)
    return group_rows(combine_groups(own_shard))


def solution(mesh):
    return jax.shard_map(
        local,
        mesh=mesh,
        in_specs=(
            P(("grp", "dp"), None, None, None),
            P(("grp", "dp"), None, None, None),
            P(),
            P(),
            P(),
        ),
        out_specs=P("grp", "dp"),
        check_vma=False,
    )
```

profile of v0, /device:TPU:1, one launch (start us, length us, event | category | flops | bytes accessed | tf_op | source)
XLA Modules:
  0.0 1404.2 jit_solution(2190759686969417998)
XLA Ops:
  6.5 2.4 fusion.15
  8.9 1.2 fusion.16
  10.1 1.3 convert_element_type.57
  11.5 5.0 fusion.14
  16.8 0.8 copy-done
  17.6 0.9 fusion.6
  18.6 6.4 multiply_reduce_fusion
  25.0 1.0 fusion.12
  26.0 7.5 concatenate.33
  33.6 1.3 dynamic-slice
  35.5 351.5 %all-reduce.8.cloned.1.call-done = f32[52,3072]{1,0:T(8,128)} async-done(((f32[52,3072]{1,0:T(8,128)}), f32[52,3072]{1,0:T(8,128)}) %all-reduce.8.cloned.1.call-update) | async-done | bytes 638992
  387.0 0.9 constant_dynamic-slice_fusion
  387.9 3.1 collective-permute-start
  391.0 1.5 collective-permute-done
  392.5 1.0 multiply_reduce_fusion.31
  394.2 0.7 slice_reduce_fusion.4
  396.3 0.8 maximum_bitcast_fusion.1
  397.0 0.7 maximum_bitcast_fusion.2
  397.8 493.3 %psum.14 = f32[3,4]{1,0:T(4,128)S(1)} all-reduce(f32[3,4]{1,0:T(4,128)S(1)} %pad_maximum_fusion), channel_id=1, replica_groups=mesh['grp'=4,'dp'=256] {'dp'}, use_global_device_ids=true, to_apply=%region_39.40 | all-reduce | flops 12 | bytes 96 | tf_op jit(solution)/shard_map/psum | solution.py:98
  891.5 4.6 collective-permute-start.1
  896.1 1.5 collective-permute-done.1
  900.5 0.8 maximum_bitcast_fusion.4
  901.2 0.7 maximum_bitcast_fusion.5
  902.0 494.3 %psum.15 = f32[3,4]{1,0:T(4,128)S(1)} all-reduce(f32[3,4]{1,0:T(4,128)S(1)} %pad_maximum_fusion.1), channel_id=1, replica_groups=mesh['grp'=4,'dp'=256] {'dp'}, use_global_device_ids=true, to_apply=%region_46.47 | all-reduce | flops 12 | bytes 96 | tf_op jit(solution)/shard_map/psum | solution.py:98
  (43 shorter events, 6.8 us)
Async XLA Ops:
  6.5 4.9 copy-start.3
  6.5 380.5 %all-reduce.8.cloned.1.call-start = ((), (), s32[]{:S(2)}) async-start(), calls=%async_computation | async-start | bytes 1376256
  16.4 1.2 copy-start
  16.4 1.2 copy-start.2
  18.6 6.4 copy-start.1
  387.9 4.6 collective-permute-start
  891.5 6.1 collective-permute-start.1
Sparse Core Ops, SparseCore 0:
  33.7 353.2 all-reduce.7
where the time goes:
time: 1400 us
  blocking collectives  988 us (71%)
  waiting for transfers between devices  354 us (25%)
  other arithmetic  25 us (2%)
  local copies, waits for them, and re-layouts  15.3 us (1%)
  between operations  14.2 us (1%)
    psum x2, blocking collectives, combine_groups(): layer_sums = lax.psum(layer_sums, 'dp')  988 us
    unnamed x2, waiting for transfers between devices  352 us
  transfers between devices with their start and end apart: 3, of which 3 were waited for; matrix products, arithmetic and copies ran while one was open for 0% of the time, Pallas kernels for 0%

commit v1 on v0

v1 whole, which is shorter than its diff:
```python
import jax
import jax.numpy as jnp
from jax import lax
from jax.experimental import pallas as pl
from jax.experimental.pallas import tpu as pltpu
from jax.sharding import PartitionSpec as P

MESH = pl.DeviceIdType.MESH
F32 = jnp.float32

NX, NY, NZ, NC = 4, 8, 16, 2
D = 3072
CELLS = 9
CROPS = 16
LANE = 128
TILES = D // LANE
CHUNK = D // NY
CT = CHUNK // LANE
PIECES = 4
PIECE = D // PIECES
OWNERS = 12
HALF_ROWS = 14
TAP0 = 8
TAPN = 40


def dp_index(y, z, c):
    return (z * NY + y) * NC + c


def pack_rows(parts, sub):
    low = sub < 4
    quads = []
    for i in range(4):
        a, b = parts[i], parts[i + 4]
        quads.append(jnp.where(low, a, b) + pltpu.roll(jnp.where(low, b, a), 4, 0))
    low = sub % 4 < 2
    pairs = []
    for i in range(2):
        a, b = quads[i], quads[i + 2]
        pairs.append(jnp.where(low, a + pltpu.roll(a, 6, 0), b + pltpu.roll(b, 2, 0)))
    a, b = pairs
    return jnp.where(sub % 2 == 0, a + pltpu.roll(a, 7, 0), b + pltpu.roll(b, 1, 0))


def kernel(
    x_hbm, u_hbm, k_hbm, b_hbm, g_hbm, out_ref,
    xv, uv, kv, bv, gv, dv, stat,
    own, half, summed, plane, acc, line, mine, gram1, got1, gram2, got2, rows,
    x_sem, u_sem, k_sem, half_s, half_r, plane_s, plane_r, line_s, line_r,
    got1_s, got1_r, got2_s, got2_r, rows_s, rows_r,
):
    me_x = lax.axis_index("grp")
    dp = lax.axis_index("dp")
    me_c = dp % NC
    me_y = dp // NC % NY
    me_z = dp // (NC * NY)

    def remote(src, dst, send, recv, x, y, z, c):
        return pltpu.make_async_remote_copy(
            src_ref=src, dst_ref=dst, send_sem=send, recv_sem=recv,
            device_id=(x, dp_index(y, z, c)), device_id_type=MESH,
        )

    def take(ref, sem):
        pltpu.make_async_copy(ref, ref, sem).wait()

    k_copies = [
        pltpu.make_async_copy(k_hbm.at[pl.ds(TAP0, TAPN)], kv, k_sem.at[0]),
        pltpu.make_async_copy(b_hbm, bv, k_sem.at[1]),
        pltpu.make_async_copy(g_hbm, gv, k_sem.at[2]),
    ]
    x_copies = [
        pltpu.make_async_copy(
            x_hbm.at[:, :, pl.ds(i * PIECE, PIECE)], xv.at[:, :, pl.ds(i * PIECE, PIECE)], x_sem.at[i]
        )
        for i in range(PIECES)
    ]
    u_copy = pltpu.make_async_copy(u_hbm, uv, u_sem)
    k_copies[0].start()
    k_copies[1].start()
    for copy in x_copies:
        copy.start()
    k_copies[2].start()
    u_copy.start()

    rows[...] = jnp.zeros_like(rows)

    barrier = pltpu.get_barrier_semaphore()

    def tell(x, y, z, c):
        pl.semaphore_signal(barrier, inc=1, device_id=(x, dp_index(y, z, c)), device_id_type=MESH)

    tell(me_x, me_y, me_z, 1 - me_c)

    @pl.loop(1, NX * NY)
    def _(n):
        tell((me_x + n // NY) % NX, (me_y + n % NY) % NY, me_z, me_c)

    @pl.loop(1, NZ)
    def _(n):
        tell(me_x, me_y, (me_z + n) % NZ, me_c)

    k_copies[0].wait()
    k_copies[1].wait()

    def conv_tile(k, carry):
        lanes = pl.ds(pl.multiple_of(k * LANE, LANE), LANE)
        cells = [xv[q, :, lanes].astype(F32) for q in range(CELLS)]
        taps = {}
        for i in range(-2, 3):
            for j in range(-2, 3):
                row = (i + 3) * 7 + j + 3 - TAP0
                taps[i, j] = kv[row : row + 1, lanes]
        bias = bv[:, lanes]
        for p in range(CELLS):
            total = None
            for q in range(CELLS):
                term = taps[q // 3 - p // 3, q % 3 - p % 3] * cells[q]
                total = term + bias if total is None else total + term
            dv[p, :, lanes] = total
        return carry

    for i in range(PIECES):
        x_copies[i].wait()
        lax.fori_loop(i * TILES // PIECES, (i + 1) * TILES // PIECES, conv_tile, 0)

    def sum_tile(k, sums):
        sums = list(sums)
        for n in range(4):
            lanes = pl.ds(pl.multiple_of((k * 4 + n) * LANE, LANE), LANE)
            for p in range(CELLS):
                sums[p] = sums[p] + dv[p, :, lanes]
        return tuple(sums)

    zero = jnp.zeros((CROPS, LANE), F32)
    sums = lax.fori_loop(0, TILES // 4, sum_tile, (zero,) * CELLS)
    means = [jnp.sum(s, 1, keepdims=True) * (1.0 / D) for s in sums]
    k_copies[2].wait()
    u_copy.wait()
    for first in range(0, CELLS, 3):

        def stat_tile(k, sums, first=first):
            sums = list(sums)
            for n in range(4):
                lanes = pl.ds(pl.multiple_of((k * 4 + n) * LANE, LANE), LANE)
                gain = gv[:, lanes]
                for i in range(3):
                    p = first + i
                    d = dv[p, :, lanes] - means[p]
                    dv[p, :, lanes] = d
                    s = uv[p, :, lanes].astype(F32) * gain
                    sums[3 * i] = sums[3 * i] + d * d
                    sums[3 * i + 1] = sums[3 * i + 1] + s
                    sums[3 * i + 2] = sums[3 * i + 2] + s * d
            return tuple(sums)

        sums = lax.fori_loop(0, TILES // 4, stat_tile, (zero,) * 9)
        for i in range(3):
            var, mean_s, mean_sd = [jnp.sum(s, 1, keepdims=True) * (1.0 / D) for s in sums[3 * i : 3 * i + 3]]
            scale = lax.rsqrt(var + 1e-06)
            stat[0, first + i] = jnp.broadcast_to(scale, (CROPS, LANE))
            stat[1, first + i] = jnp.broadcast_to(scale * mean_s, (CROPS, LANE))
            stat[2, first + i] = jnp.broadcast_to(scale * scale * scale * mean_sd, (CROPS, LANE))

    sub = lax.broadcasted_iota(jnp.int32, (8, LANE), 0)

    def grad_tile(y, t):
        lanes = pl.ds(pl.multiple_of(y * CHUNK + t * LANE, LANE), LANE)
        gain = gv[:, lanes]
        grads = []
        sum_g = sum_ud = sum_u = None
        for p in range(CELLS):
            d = dv[p, :, lanes]
            u = uv[p, :, lanes].astype(F32)
            scale = stat[0, p]
            grad = u * gain * scale - stat[1, p] - d * stat[2, p]
            ud = u * (d * scale)
            grads.append(grad)
            sum_g = grad if p == 0 else sum_g + grad
            sum_ud = ud if p == 0 else sum_ud + ud
            sum_u = u if p == 0 else sum_u + u
        cells = [xv[q, :, lanes].astype(F32) for q in range(CELLS)]
        parts = []
        for i in range(-2, 3):
            for j in range(-2, 3):
                total = None
                for p in range(CELLS):
                    a, b = p // 3 + i, p % 3 + j
                    if 0 <= a < 3 and 0 <= b < 3:
                        term = grads[p] * cells[3 * a + b]
                        total = term if total is None else total + term
                parts.append(total)
        parts += [sum_g, sum_ud, sum_u]
        parts = [v[:8] + v[8:] for v in parts]
        none = jnp.zeros((8, LANE), F32)
        for c in range(NC):
            group = parts[c * HALF_ROWS : (c + 1) * HALF_ROWS] + [none, none]
            for h in range(2):
                packed = pack_rows(group[8 * h : 8 * h + 8], sub)
                own[y, c, 2 * h, t] = packed[:4]
                own[y, c, 2 * h + 1, t] = packed[4:]

    def chunk_of(i):
        off = jnp.where(i % 2 == 0, 4 + i // 2, 4 - (i + 1) // 2)
        return (me_y + off) % NY

    def half_copy(i):
        return remote(
            own.at[chunk_of(i), 1 - me_c], half.at[i], half_s.at[i], half_r.at[i], me_x, me_y, me_z, 1 - me_c
        )

    me_slot = me_x * NY + me_y

    def add_half(i):
        half_copy(i).wait_recv()
        y = chunk_of(i)
        for x in range(NX):
            for t in range(CT):
                summed[i, x, t] = own[y, me_c, x, t] + half[i, x, t]

    def plane_copy(i, x):
        return remote(
            summed.at[i, x], plane.at[me_slot], plane_s, plane_r, x, chunk_of(i), me_z, me_c
        )

    pl.semaphore_wait(barrier, NX * NY + NZ - 1)

    @pl.loop(0, NY)
    def _(i):
        y = chunk_of(i)

        @pl.loop(0, CT)
        def _(t):
            grad_tile(y, t)

        half_copy(i).start()

        @pl.when(i > 0)
        def _():
            add_half(i - 1)
            for n in range(NX):
                plane_copy(i - 1, (me_x + 2 + n) % NX).start()

    add_half(NY - 1)
    for n in (2, 1, 3):
        plane_copy(NY - 1, (me_x + n) % NX).start()
    for t in range(CT):
        plane[me_slot, t] = summed[NY - 1, me_x, t]

    take(plane.at[pl.ds(0, NX * NY - 1)], plane_r)
    for g in range(NX):
        for t in range(CT):
            total = plane[g * NY, t]
            for y in range(1, NY):
                total = total + plane[g * NY + y, t]
            for j in range(4):
                acc[t * 4 + j, g : g + 1] = total[j : j + 1]

    def line_copy(z):
        return remote(acc.at[z], line.at[me_z], line_s, line_r, me_x, me_y, z, me_c)

    @pl.loop(1, NZ)
    def _(n):
        off = jnp.where(n % 2 == 0, 8 + n // 2, 8 - n // 2)
        z = (me_z + off) % NZ

        @pl.when(z < OWNERS)
        def _():
            line_copy(z).start()

    owner = me_z < OWNERS
    tile = me_z // 4
    slot = me_x * 4 + me_z % 4
    rho = me_c * HALF_ROWS + slot
    real = owner & (slot < HALF_ROWS)
    layer = jnp.maximum(rho - 24, 0)
    row_abs = jnp.where(rho < 25, 7 * (rho // 5 + 1) + rho % 5 + 1, rho + 24)
    first = tile * 32 // 3

    def dest(n):
        e = first + n
        ok = real & (e < 32) & (12 * e < LANE * (tile + 1))
        x = row_abs // 13
        to = (x, dp_index(e % 16 // 2, 2 * me_y + e // 16, e % 2))
        at = row_abs % 13 * 2 + tile - 12 * e // LANE
        here = (x == me_x) & (to[1] == dp)
        return ok, here, to, at

    def row_copy(n):
        _, _, to, at = dest(n)
        return pltpu.make_async_remote_copy(
            src_ref=mine, dst_ref=rows.at[at], send_sem=rows_s.at[n], recv_sem=rows_r,
            device_id=to, device_id_type=MESH,
        )

    def gram1_copy(n):
        return remote(
            gram1, got1.at[me_z * NC + me_c], got1_s, got1_r, me_x, me_y, (me_z + n // NC) % NZ, (me_c + n % NC) % NC
        )

    @pl.when(owner)
    def _():
        line[me_z] = acc[me_z]
        take(line.at[pl.ds(0, NZ - 1)], line_r)
        total = line[0]
        for z in range(1, NZ):
            total = total + line[z]
        mine[...] = total
        lane = lax.broadcasted_iota(jnp.int32, (4, LANE), 1)
        row = lax.broadcasted_iota(jnp.int32, (4, LANE), 0)
        gram = jnp.zeros((4, LANE), F32)
        for g in range(NX):
            dots = jnp.sum(total * total[g : g + 1], 1, keepdims=True)
            gram = gram + jnp.where(lane == layer * 16 + g * 4 + row, dots, 0.0)
        gram1[...] = jnp.sum(gram, 0, keepdims=True)

        @pl.loop(1, NZ * NC)
        def _(n):
            gram1_copy(n).start()

        got1[me_z * NC + me_c] = gram1[...]

        @pl.loop(0, 12)
        def _(n):
            ok, here, to, at = dest(n)

            @pl.when(ok & here)
            def _():
                pltpu.make_async_copy(mine, rows.at[at], rows_r).start()

            @pl.when(ok & jnp.logical_not(here))
            def _():
                row_copy(n).start()

        take(got1.at[pl.ds(0, OWNERS * NC - 1)], got1_r)

    @pl.when(jnp.logical_not(owner))
    def _():
        take(got1.at[pl.ds(0, OWNERS * NC)], got1_r)

    total = got1[0]
    for n in range(1, OWNERS * NC):
        total = total + got1[n]
    gram2[...] = total

    def gram2_copy(n):
        return remote(
            gram2, got2.at[me_slot], got2_s, got2_r, (me_x + n // NY) % NX, (me_y + n % NY) % NY, me_z, me_c
        )

    @pl.loop(1, NX * NY)
    def _(n):
        gram2_copy(n).start()

    got2[me_slot] = gram2[...]
    take(got2.at[pl.ds(0, NX * NY - 1)], got2_r)
    total = got2[0]
    for n in range(1, NX * NY):
        total = total + got2[n]

    def entry(k):
        return total if k == 0 else pltpu.roll(total, LANE - k, 1)

    n0, p01, p02, p03, n1, p12, p13, n2, p23, n3 = [entry(k) for k in (0, 1, 2, 3, 5, 6, 7, 10, 11, 15)]
    a0 = 1.0 - p01 / (2.0 * n0)
    a1 = 1.0 - p01 / (2.0 * n1)
    a2 = 1.0 - p23 / (2.0 * n2)
    a3 = 1.0 - p23 / (2.0 * n3)
    inner = a0 * (a2 * p02 + a3 * p03) + a1 * (a2 * p12 + a3 * p13)
    low = a0 * (a0 * n0 + a1 * p01) + a1 * (a0 * p01 + a1 * n1)
    high = a2 * (a2 * n2 + a3 * p23) + a3 * (a2 * p23 + a3 * n3)
    lo = 1.0 - inner / (2.0 * low)
    hi = 1.0 - inner / (2.0 * high)
    coeffs = jnp.concatenate([lo * a0, lo * a1, hi * a2, hi * a3], 0)
    lane = lax.broadcasted_iota(jnp.int32, (4, LANE), 1)
    by_layer = [
        jnp.sum(jnp.where(lane == 16 * n, coeffs, 0.0), 1, keepdims=True) for n in range(4)
    ]

    place = me_z % 2 * 16 + me_y * 2 + me_c
    lanes_off = 12 * place % LANE
    straddles = lanes_off + 12 > LANE
    many = (me_x == 1) | (me_x == 2)
    for is_many, is_two, count in ((False, False, 5), (True, False, 9), (False, True, 10), (True, True, 18)):

        @pl.when((many == is_many) & (straddles == is_two))
        def _(count=count):
            take(rows.at[pl.ds(0, count)], rows_r)

    blended = [[], []]
    for p in range(13):
        coeff = by_layer[0]
        if p >= 10:
            coeff = jnp.where(me_x == NX - 1, by_layer[p - 9], coeff)
        for t in range(2):
            blended[t].append(jnp.sum(rows[2 * p + t] * coeff, 0, keepdims=True))
    shift = (LANE - lanes_off) % LANE
    first_tile, second_tile = [pltpu.roll(jnp.concatenate(b, 0), shift, 1) for b in blended]
    lane = lax.broadcasted_iota(jnp.int32, (13, LANE), 1)
    out_ref[...] = jnp.where(lane + lanes_off < LANE, first_tile, second_tile)[:, :12]

    @pl.loop(0, NY)
    def _(i):
        half_copy(i).wait_send()

    take(plane.at[pl.ds(0, NX * NY - 1)], plane_s)
    take(got2.at[pl.ds(0, NX * NY - 1)], got2_s)

    @pl.when(owner)
    def _():
        take(line.at[pl.ds(0, OWNERS - 1)], line_s)
        take(got2.at[pl.ds(0, NZ * NC - 1)], got1_s)

    @pl.when(jnp.logical_not(owner))
    def _():
        take(line.at[pl.ds(0, OWNERS)], line_s)

    @pl.loop(0, 12)
    def _(n):
        ok, here, to, at = dest(n)

        @pl.when(ok & jnp.logical_not(here))
        def _():
            row_copy(n).wait_send()


def local(crops_in, cotangent, kern, conv_bias, norm_gain):
    cells = jnp.transpose(crops_in, (1, 2, 0, 3)).reshape(CELLS, CROPS, D)
    cots = jnp.transpose(cotangent, (1, 2, 0, 3)).reshape(CELLS, CROPS, D)
    bf16 = jnp.bfloat16
    vmem = pltpu.VMEM
    dma = pltpu.SemaphoreType.DMA
    return pl.pallas_call(
        kernel,
        out_shape=jax.ShapeDtypeStruct((13, 12), F32),
        in_specs=[pl.BlockSpec(memory_space=pl.ANY)] * 5,
        out_specs=pl.BlockSpec(memory_space=pltpu.VMEM),
        scratch_shapes=[
            vmem((CELLS, CROPS, D), bf16),
            vmem((CELLS, CROPS, D), bf16),
            vmem((TAPN, D), F32),
            vmem((1, D), F32),
            vmem((1, D), F32),
            vmem((CELLS, CROPS, D), F32),
            vmem((3, CELLS, CROPS, LANE), F32),
            vmem((NY, NC, NX, CT, 4, LANE), F32),
            vmem((NY, NX, CT, 4, LANE), F32),
            vmem((NY, NX, CT, 4, LANE), F32),
            vmem((NX * NY, CT, 4, LANE), F32),
            vmem((OWNERS, NX, LANE), F32),
            vmem((NZ, NX, LANE), F32),
            vmem((NX, LANE), F32),
            vmem((1, LANE), F32),
            vmem((OWNERS * NC, 1, LANE), F32),
            vmem((1, LANE), F32),
            vmem((NX * NY, 1, LANE), F32),
            vmem((26, NX, LANE), F32),
            dma((PIECES,)),
            dma,
            dma((3,)),
            dma((NY,)),
            dma((NY,)),
            dma, dma, dma, dma, dma, dma, dma, dma,
            dma((12,)),
            dma,
        ],
        compiler_params=pltpu.CompilerParams(
            collective_id=0, has_side_effects=True, vmem_limit_bytes=48 * 1024 * 1024
        ),
    )(cells, cots, kern, conv_bias.reshape(1, D), norm_gain.reshape(1, D))


def solution(mesh):
    return jax.shard_map(
        local,
        mesh=mesh,
        in_specs=(
            P(("grp", "dp"), None, None, None),
            P(("grp", "dp"), None, None, None),
            P(),
            P(),
            P(),
        ),
        out_specs=P("grp", "dp"),
        check_vma=False,
    )
```

time: 1400 us -> 60.2 us (0.04)
  blocking collectives: 988 us -> 0 us
  waiting for transfers between devices: 354 us -> 0 us
  Pallas kernels: 0 us -> 54.3 us
  other arithmetic: 25 us -> 0 us
  between operations: 14.2 us -> 0.01 us
    psum x2 -> x0, blocking collectives: 988 us -> none  [combine_groups(): layer_sums = lax.psum(layer_sums, 'dp')]
    unnamed x2 -> x0, waiting for transfers between devices: 352 us -> none
    pallas_call x0 -> x1, Pallas kernels: none -> 54.3 us  [local(): pl.pallas_call(kernel, out_shape=jax.ShapeDtypeStruct((13, 12), F32), in_...]
    reduce_sum x13 -> x0, other arithmetic: 18.6 us -> none  [the longest x1 6.42 us: block_bucket(): jnp.sum(grad_conv * shifted(inputs, row_off, col_off), (0, 1, 2))]
  transfers between devices with their start and end apart: 3 -> 0, of which waited for: 3 -> 0; matrix products, arithmetic and copies ran while one was open for 0% -> 0% of each run, Pallas kernels for 0% -> 0%
where the time goes in v1:
time: 60.2 us; the launch traced here: 59.8 us
  Pallas kernels  54.3 us (90%)
  local copies, waits for them, and re-layouts  5.45 us (9%)
    pallas_call x1, Pallas kernels, local(): pl.pallas_call(kernel, out_shape=jax.ShapeDtypeStruct((13, 12), F32), in_...  54.3 us
    unnamed x11, local copies, waits for them, and re-layouts  5.45 us

profile of v1, /device:TPU:1, one launch (start us, length us, event | category | flops | bytes accessed | tf_op | source)
XLA Modules:
  0.0 59.8 jit_solution(654441447285905653)
XLA Ops:
  0.0 0.0 copy-start
  0.0 1.2 %copy-done = bf16[16,3,3,3072]{3,0,2,1:T(8,128)(2,1)S(1)} copy-done((bf16[16,3,3,3072]{3,0,2,1:T(8,128)(2,1)S(1)}, bf16[16,3,3,3072]{3,0,2,1:T(8,128)(2,1)}, u32[]{:S(2)}) %copy-start) | copy-done | bytes 884760
  1.2 0.0 copy-start.1
  1.2 1.2 %copy-done.1 = bf16[16,3,3,3072]{3,0,2,1:T(8,128)(2,1)S(1)} copy-done((bf16[16,3,3,3072]{3,0,2,1:T(8,128)(2,1)S(1)}, bf16[16,3,3,3072]{3,0,2,1:T(8,128)(2,1)}, u32[]{:S(2)}) %copy-start.1) | copy-done | bytes 884760
  2.3 0.0 copy-start.2
  2.3 1.1 %copy-done.2 = f32[49,3072]{1,0:T(8,128)S(1)} copy-done((f32[49,3072]{1,0:T(8,128)S(1)}, f32[49,3072]{1,0:T(8,128)}, u32[]{:S(2)}) %copy-start.2) | copy-done | bytes 602136
  3.4 0.0 copy-start.3
  3.4 0.7 %copy-done.3 = f32[3072]{0:T(1024)S(1)} copy-done((f32[3072]{0:T(1024)S(1)}, f32[3072]{0:T(1024)}, u32[]{:S(2)}) %copy-start.3) | copy-done | bytes 12312
  4.1 0.0 copy-start.4
  4.1 0.7 %copy-done.4 = f32[3072]{0:T(1024)S(1)} copy-done((f32[3072]{0:T(1024)S(1)}, f32[3072]{0:T(1024)}, u32[]{:S(2)}) %copy-start.4) | copy-done | bytes 12312
  4.9 54.3 %shard_map.55 = f32[13,12]{1,0:T(8,128)S(1)} custom-call(bf16[9,16,3072]{2,1,0:T(8,128)(2,1)S(1)} %bitcast.8, bf16[9,16,3072]{2,1,0:T(8,128)(2,1)S(1)} %bitcast.9, f32[49,3072]{1,0:T(8,128)S(1)} %copy-done.2, f32[1,3072]{1,0:T(1,128)S(1)} %bitcast.10, f32[1,3072]{1,0:T(1,128)S(1)} %bitcast.11), custom_call_target="tpu_custom_call" | custom-call | tf_op jit(solution)/shard_map/pallas_call | solution.py:434
  59.2 0.6 %copy.7 = f32[13,12]{1,0:T(8,128)} copy(f32[13,12]{1,0:T(8,128)S(1)} %shard_map.55) | data formatting | bytes 1248
Async XLA Ops:
  0.0 1.2 %copy-start = (bf16[16,3,3,3072]{3,0,2,1:T(8,128)(2,1)S(1)}, bf16[16,3,3,3072]{3,0,2,1:T(8,128)(2,1)}, u32[]{:S(2)}) copy-start(bf16[16,3,3,3072]{3,0,2,1:T(8,128)(2,1)} %param.5) | copy-start | bytes 2654212
  1.2 1.2 %copy-start.1 = (bf16[16,3,3,3072]{3,0,2,1:T(8,128)(2,1)S(1)}, bf16[16,3,3,3072]{3,0,2,1:T(8,128)(2,1)}, u32[]{:S(2)}) copy-start(bf16[16,3,3,3072]{3,0,2,1:T(8,128)(2,1)} %param.6) | copy-start | bytes 2654212
  2.3 1.1 %copy-start.2 = (f32[49,3072]{1,0:T(8,128)S(1)}, f32[49,3072]{1,0:T(8,128)}, u32[]{:S(2)}) copy-start(f32[49,3072]{1,0:T(8,128)} %k_hbm.1) | copy-start | bytes 1806340
  3.4 0.7 %copy-start.3 = (f32[3072]{0:T(1024)S(1)}, f32[3072]{0:T(1024)}, u32[]{:S(2)}) copy-start(f32[3072]{0:T(1024)} %param.8) | copy-start | bytes 36868
  4.1 0.7 %copy-start.4 = (f32[3072]{0:T(1024)S(1)}, f32[3072]{0:T(1024)}, u32[]{:S(2)}) copy-start(f32[3072]{0:T(1024)} %param.9) | copy-start | bytes 36868

commit v2 on v1

--- a/solution.py
+++ b/solution.py
@@ -18,10 +18,34 @@
 CT = CHUNK // LANE
 PIECES = 4
 PIECE = D // PIECES
-OWNERS = 12
-HALF_ROWS = 14
 TAP0 = 8
 TAPN = 40
+START = (0, 6, 14, 22)
+COUNT = (3, 4, 4, 3)
+ROW_OF = [7 * (r // 5 + 1) + r % 5 + 1 for r in range(25)] + [49, 50, 51]
+
+
+def out_rows():
+    found = [[] for _ in range(NX)]
+    for x in range(NX):
+        for c in range(NC):
+            for j in range(COUNT[x]):
+                row = ROW_OF[START[x] + c * COUNT[x] + j]
+                found[row // 13].append((row % 13, c if row // 13 == x else 2, j))
+    return found
+
+
+OUT_ROWS = out_rows()
+TILES_OF = [sorted({12 * e // LANE, (12 * e + 11) // LANE}) for e in range(2 * NY * NC)]
+SENDS = sum(len(t) for t in TILES_OF)
+
+
+def ring(n, size):
+    return min(n, size - n)
+
+
+FAR = sorted(range(1, NX * NY), key=lambda i: -ring(i // NY, NX) - ring(i % NY, NY))
+FAR_HUB = sorted(range(1, NX * NY * NC), key=lambda i: -2 * ring(i // 16, NX) - ring(i % 16, 16))
 
 
 def dp_index(y, z, c):
@@ -46,9 +70,9 @@
 def kernel(
     x_hbm, u_hbm, k_hbm, b_hbm, g_hbm, out_ref,
     xv, uv, kv, bv, gv, dv, stat,
-    own, half, summed, plane, acc, line, mine, gram1, got1, gram2, got2, rows,
+    own, half, summed, plane, acc, line, both, part, parts_in, gram, rows, ruler,
     x_sem, u_sem, k_sem, half_s, half_r, plane_s, plane_r, line_s, line_r,
-    got1_s, got1_r, got2_s, got2_r, rows_s, rows_r,
+    parts_s, parts_r, total_s, total_r, rows_s, rows_r,
 ):
     me_x = lax.axis_index("grp")
     dp = lax.axis_index("dp")
@@ -84,22 +108,25 @@
     k_copies[2].start()
     u_copy.start()
 
-    rows[...] = jnp.zeros_like(rows)
-
+    def turn(v, n, size):
+        return v if n == 0 else jnp.where(v + n >= size, v + n - size, v + n)
+
+    near_x = [turn(me_x, n, NX) for n in range(NX)]
+    near_y = [turn(me_y, n, NY) for n in range(NY)]
     barrier = pltpu.get_barrier_semaphore()
 
     def tell(x, y, z, c):
         pl.semaphore_signal(barrier, inc=1, device_id=(x, dp_index(y, z, c)), device_id_type=MESH)
 
+    for i in FAR:
+        tell(near_x[i // NY], near_y[i % NY], me_z, me_c)
     tell(me_x, me_y, me_z, 1 - me_c)
-
-    @pl.loop(1, NX * NY)
-    def _(n):
-        tell((me_x + n // NY) % NX, (me_y + n % NY) % NY, me_z, me_c)
-
-    @pl.loop(1, NZ)
-    def _(n):
-        tell(me_x, me_y, (me_z + n) % NZ, me_c)
+    hub = me_z == 0
+
+    @pl.when(hub)
+    def _():
+        for z in range(NZ - 1, 0, -1):
+            tell(me_x, me_y, z, me_c)
 
     k_copies[0].wait()
     k_copies[1].wait()
@@ -195,7 +222,9 @@
         parts = [v[:8] + v[8:] for v in parts]
         none = jnp.zeros((8, LANE), F32)
         for c in range(NC):
-            group = parts[c * HALF_ROWS : (c + 1) * HALF_ROWS] + [none, none]
+            group = []
+            for x in range(NX):
+                group += parts[START[x] + c * COUNT[x] : START[x] + (c + 1) * COUNT[x]] + [none] * (4 - COUNT[x])
             for h in range(2):
                 packed = pack_rows(group[8 * h : 8 * h + 8], sub)
                 own[y, c, 2 * h, t] = packed[:4]
@@ -224,7 +253,7 @@
             summed.at[i, x], plane.at[me_slot], plane_s, plane_r, x, chunk_of(i), me_z, me_c
         )
 
-    pl.semaphore_wait(barrier, NX * NY + NZ - 1)
+    pl.semaphore_wait(barrier, NX * NY + jnp.where(hub, 0, 1))
 
     @pl.loop(0, NY)
     def _(i):
@@ -239,12 +268,12 @@
         @pl.when(i > 0)
         def _():
             add_half(i - 1)
-            for n in range(NX):
-                plane_copy(i - 1, (me_x + 2 + n) % NX).start()
+            for n in (2, 1, 3, 0):
+                plane_copy(i - 1, near_x[n]).start()
 
     add_half(NY - 1)
     for n in (2, 1, 3):
-        plane_copy(NY - 1, (me_x + n) % NX).start()
+        plane_copy(NY - 1, near_x[n]).start()
     for t in range(CT):
         plane[me_slot, t] = summed[NY - 1, me_x, t]
 
@@ -254,110 +283,91 @@
             total = plane[g * NY, t]
             for y in range(1, NY):
                 total = total + plane[g * NY + y, t]
-            for j in range(4):
-                acc[t * 4 + j, g : g + 1] = total[j : j + 1]
-
-    def line_copy(z):
-        return remote(acc.at[z], line.at[me_z], line_s, line_r, me_x, me_y, z, me_c)
-
-    @pl.loop(1, NZ)
-    def _(n):
-        off = jnp.where(n % 2 == 0, 8 + n // 2, 8 - n // 2)
-        z = (me_z + off) % NZ
-
-        @pl.when(z < OWNERS)
+            acc[t, g] = total
+
+    line_copy = remote(acc, line.at[me_z], line_s, line_r, me_x, me_y, 0, me_c)
+
+    def total_copy(z):
+        return remote(gram, gram, total_s, total_r, me_x, me_y, z, me_c)
+
+    odd_low = (me_x == 0) & (me_c == 1)
+    odd_high = (me_x == NX - 1) & (me_c == 0)
+    odd = odd_low | odd_high
+    odd_x = jnp.where(odd_low, 1, NX - 2)
+    row4 = lax.broadcasted_iota(jnp.int32, (4, LANE), 0)
+    lane4 = lax.broadcasted_iota(jnp.int32, (4, LANE), 1)
+
+    def row_copy(t, place, x, e):
+        return pltpu.make_async_remote_copy(
+            src_ref=both.at[t], dst_ref=rows.at[place], send_sem=rows_s, recv_sem=rows_r,
+            device_id=(x, 2 * NY * NC * me_y + e), device_id_type=MESH,
+        )
+
+    @pl.when(jnp.logical_not(hub))
+    def _():
+        line_copy.start()
+        take(gram, total_r)
+
+    @pl.when(hub)
+    def _():
+        take(line.at[pl.ds(1, NZ - 1)], line_r)
+        sums = []
+        for t in range(CT):
+            of_tile = []
+            for g in range(NX):
+                total = acc[t, g]
+                for z in range(1, NZ):
+                    total = total + line[z, t, g]
+                both[t, g] = total
+                of_tile.append(total)
+            sums.append(of_tile)
+        layer = jnp.where((me_x == NX - 1) & (me_c == 1), row4 + 1, 0)
+        dots = jnp.zeros((4, LANE), F32)
+        for g in range(NX):
+            for h in range(g, NX):
+                dot = sum(sums[t][g] * sums[t][h] for t in range(CT))
+                dot = jnp.sum(dot, 1, keepdims=True)
+                dots = dots + jnp.where(lane4 == layer * 16 + 4 * g + h, dot, 0.0)
+        part[...] = jnp.sum(dots, 0, keepdims=True)
+        slot = me_x * (NY * NC) + dp
+        near_dp = [turn(dp, n, NY * NC) for n in range(NY * NC)]
+        for i in FAR_HUB:
+            pltpu.make_async_remote_copy(
+                src_ref=part, dst_ref=parts_in.at[slot], send_sem=parts_s, recv_sem=parts_r,
+                device_id=(near_x[i // (NY * NC)], near_dp[i % (NY * NC)]), device_id_type=MESH,
+            ).start()
+        parts_in[slot] = part[...]
+
+        for e in range(2 * NY * NC):
+            for n, t in enumerate(TILES_OF[e]):
+                if e < NC:
+                    here = (me_y == 0) & (me_c == e)
+
+                    @pl.when(here)
+                    def _(t=t, n=n):
+                        pltpu.make_async_copy(both.at[t], rows.at[2 * me_c + n], rows_r).start()
+
+                    @pl.when(jnp.logical_not(here))
+                    def _(t=t, n=n, e=e):
+                        row_copy(t, 2 * me_c + n, me_x, e).start()
+                else:
+                    row_copy(t, 2 * me_c + n, me_x, e).start()
+
+        @pl.when(odd)
         def _():
-            line_copy(z).start()
-
-    owner = me_z < OWNERS
-    tile = me_z // 4
-    slot = me_x * 4 + me_z % 4
-    rho = me_c * HALF_ROWS + slot
-    real = owner & (slot < HALF_ROWS)
-    layer = jnp.maximum(rho - 24, 0)
-    row_abs = jnp.where(rho < 25, 7 * (rho // 5 + 1) + rho % 5 + 1, rho + 24)
-    first = tile * 32 // 3
-
-    def dest(n):
-        e = first + n
-        ok = real & (e < 32) & (12 * e < LANE * (tile + 1))
-        x = row_abs // 13
-        to = (x, dp_index(e % 16 // 2, 2 * me_y + e // 16, e % 2))
-        at = row_abs % 13 * 2 + tile - 12 * e // LANE
-        here = (x == me_x) & (to[1] == dp)
-        return ok, here, to, at
-
-    def row_copy(n):
-        _, _, to, at = dest(n)
-        return pltpu.make_async_remote_copy(
-            src_ref=mine, dst_ref=rows.at[at], send_sem=rows_s.at[n], recv_sem=rows_r,
-            device_id=to, device_id_type=MESH,
-        )
-
-    def gram1_copy(n):
-        return remote(
-            gram1, got1.at[me_z * NC + me_c], got1_s, got1_r, me_x, me_y, (me_z + n // NC) % NZ, (me_c + n % NC) % NC
-        )
-
-    @pl.when(owner)
-    def _():
-        line[me_z] = acc[me_z]
-        take(line.at[pl.ds(0, NZ - 1)], line_r)
-        total = line[0]
+            for e in range(2 * NY * NC):
+                for n, t in enumerate(TILES_OF[e]):
+                    row_copy(t, 4 + n, odd_x, e).start()
+
+        take(parts_in.at[pl.ds(0, NX * NY * NC - 1)], parts_r)
+        totals = [parts_in[n] for n in range(4)]
+        for n in range(4, NX * NY * NC):
+            totals[n % 4] = totals[n % 4] + parts_in[n]
+        gram[...] = (totals[0] + totals[1]) + (totals[2] + totals[3])
         for z in range(1, NZ):
-            total = total + line[z]
-        mine[...] = total
-        lane = lax.broadcasted_iota(jnp.int32, (4, LANE), 1)
-        row = lax.broadcasted_iota(jnp.int32, (4, LANE), 0)
-        gram = jnp.zeros((4, LANE), F32)
-        for g in range(NX):
-            dots = jnp.sum(total * total[g : g + 1], 1, keepdims=True)
-            gram = gram + jnp.where(lane == layer * 16 + g * 4 + row, dots, 0.0)
-        gram1[...] = jnp.sum(gram, 0, keepdims=True)
-
-        @pl.loop(1, NZ * NC)
-        def _(n):
-            gram1_copy(n).start()
-
-        got1[me_z * NC + me_c] = gram1[...]
-
-        @pl.loop(0, 12)
-        def _(n):
-            ok, here, to, at = dest(n)
-
-            @pl.when(ok & here)
-            def _():
-                pltpu.make_async_copy(mine, rows.at[at], rows_r).start()
-
-            @pl.when(ok & jnp.logical_not(here))
-            def _():
-                row_copy(n).start()
-
-        take(got1.at[pl.ds(0, OWNERS * NC - 1)], got1_r)
-
-    @pl.when(jnp.logical_not(owner))
-    def _():
-        take(got1.at[pl.ds(0, OWNERS * NC)], got1_r)
-
-    total = got1[0]
-    for n in range(1, OWNERS * NC):
-        total = total + got1[n]
-    gram2[...] = total
-
-    def gram2_copy(n):
-        return remote(
-            gram2, got2.at[me_slot], got2_s, got2_r, (me_x + n // NY) % NX, (me_y + n % NY) % NY, me_z, me_c
-        )
-
-    @pl.loop(1, NX * NY)
-    def _(n):
-        gram2_copy(n).start()
-
-    got2[me_slot] = gram2[...]
-    take(got2.at[pl.ds(0, NX * NY - 1)], got2_r)
-    total = got2[0]
-    for n in range(1, NX * NY):
-        total = total + got2[n]
+            total_copy(z).start()
+
+    total = gram[...]
 
     def entry(k):
         return total if k == 0 else pltpu.roll(total, LANE - k, 1)
@@ -372,57 +382,59 @@
     high = a2 * (a2 * n2 + a3 * p23) + a3 * (a2 * p23 + a3 * n3)
     lo = 1.0 - inner / (2.0 * low)
     hi = 1.0 - inner / (2.0 * high)
-    coeffs = jnp.concatenate([lo * a0, lo * a1, hi * a2, hi * a3], 0)
-    lane = lax.broadcasted_iota(jnp.int32, (4, LANE), 1)
-    by_layer = [
-        jnp.sum(jnp.where(lane == 16 * n, coeffs, 0.0), 1, keepdims=True) for n in range(4)
-    ]
+    coeffs = [lo * a0, lo * a1, hi * a2, hi * a3]
+    layer = jnp.where(me_x == NX - 1, row4 + 1, 0)
+    first_layer = [jnp.sum(jnp.where(lane4 == 0, c, 0.0), 1, keepdims=True) for c in coeffs]
+    row_layer = [jnp.sum(jnp.where(lane4 == 16 * layer, c, 0.0), 1, keepdims=True) for c in coeffs]
 
     place = me_z % 2 * 16 + me_y * 2 + me_c
     lanes_off = 12 * place % LANE
     straddles = lanes_off + 12 > LANE
-    many = (me_x == 1) | (me_x == 2)
-    for is_many, is_two, count in ((False, False, 5), (True, False, 9), (False, True, 10), (True, True, 18)):
-
-        @pl.when((many == is_many) & (straddles == is_two))
-        def _(count=count):
-            take(rows.at[pl.ds(0, count)], rows_r)
-
-    blended = [[], []]
-    for p in range(13):
-        coeff = by_layer[0]
-        if p >= 10:
-            coeff = jnp.where(me_x == NX - 1, by_layer[p - 9], coeff)
-        for t in range(2):
-            blended[t].append(jnp.sum(rows[2 * p + t] * coeff, 0, keepdims=True))
+    inside = (me_x == 1) | (me_x == NX - 2)
+    for is_inside in (False, True):
+        for is_two in (False, True):
+
+            @pl.when((inside == is_inside) & (straddles == is_two))
+            def _(count=(2 + is_inside) * (1 + is_two)):
+                take(rows.at[pl.ds(0, count)], rows_r)
+
     shift = (LANE - lanes_off) % LANE
-    first_tile, second_tile = [pltpu.roll(jnp.concatenate(b, 0), shift, 1) for b in blended]
-    lane = lax.broadcasted_iota(jnp.int32, (13, LANE), 1)
-    out_ref[...] = jnp.where(lane + lanes_off < LANE, first_tile, second_tile)[:, :12]
+    keep = lane4 + lanes_off < LANE
+    blended = []
+    for k, coeff in enumerate((first_layer, row_layer, first_layer)):
+        by_tile = []
+        for n in range(2):
+            value = sum(rows[2 * k + n, g] * coeff[g] for g in range(NX))
+            by_tile.append(pltpu.roll(value, shift, 1))
+        blended.append(jnp.where(keep, by_tile[0], by_tile[1])[:, :12])
+    out_ref[...] = jnp.zeros_like(out_ref)
+    for x in range(NX):
+
+        @pl.when(me_x == x)
+        def _(x=x):
+            for at, k, j in OUT_ROWS[x]:
+                out_ref[at : at + 1] = blended[k][j : j + 1]
 
     @pl.loop(0, NY)
     def _(i):
         half_copy(i).wait_send()
 
     take(plane.at[pl.ds(0, NX * NY - 1)], plane_s)
-    take(got2.at[pl.ds(0, NX * NY - 1)], got2_s)
-
-    @pl.when(owner)
+
+    @pl.when(jnp.logical_not(hub))
     def _():
-        take(line.at[pl.ds(0, OWNERS - 1)], line_s)
-        take(got2.at[pl.ds(0, NZ * NC - 1)], got1_s)
-
-    @pl.when(jnp.logical_not(owner))
+        line_copy.wait_send()
+
+    @pl.when(hub)
     def _():
-        take(line.at[pl.ds(0, OWNERS)], line_s)
-
-    @pl.loop(0, 12)
-    def _(n):
-        ok, here, to, at = dest(n)
-
-        @pl.when(ok & jnp.logical_not(here))
-        def _():
-            row_copy(n).wait_send()
+        take(parts_in.at[pl.ds(0, NX * NY * NC - 1)], parts_s)
+        take(parts_in.at[pl.ds(0, NZ - 1)], total_s)
+        for is_odd in (False, True):
+            for is_first in (False, True):
+
+                @pl.when((odd == is_odd) & ((me_y == 0) == is_first))
+                def _(count=SENDS * (1 + is_odd) - is_first):
+                    take(ruler.at[pl.ds(0, count)], rows_s)
 
 
 def local(crops_in, cotangent, kern, conv_bias, norm_gain):
@@ -448,25 +460,23 @@
             vmem((NY, NX, CT, 4, LANE), F32),
             vmem((NY, NX, CT, 4, LANE), F32),
             vmem((NX * NY, CT, 4, LANE), F32),
-            vmem((OWNERS, NX, LANE), F32),
-            vmem((NZ, NX, LANE), F32),
-            vmem((NX, LANE), F32),
+            vmem((CT, NX, 4, LANE), F32),
+            vmem((NZ, CT, NX, 4, LANE), F32),
+            vmem((CT, NX, 4, LANE), F32),
             vmem((1, LANE), F32),
-            vmem((OWNERS * NC, 1, LANE), F32),
+            vmem((NX * NY * NC, 1, LANE), F32),
             vmem((1, LANE), F32),
-            vmem((NX * NY, 1, LANE), F32),
-            vmem((26, NX, LANE), F32),
+            vmem((6, NX, 4, LANE), F32),
+            vmem((2 * SENDS, NX, 4, LANE), F32),
             dma((PIECES,)),
             dma,
             dma((3,)),
             dma((NY,)),
             dma((NY,)),
-            dma, dma, dma, dma, dma, dma, dma, dma,
-            dma((12,)),
-            dma,
+            dma, dma, dma, dma, dma, dma, dma, dma, dma, dma,
         ],
         compiler_params=pltpu.CompilerParams(
-            collective_id=0, has_side_effects=True, vmem_limit_bytes=48 * 1024 * 1024
+            collective_id=0, has_side_effects=True, vmem_limit_bytes=61 * 1024 * 1024
         ),
     )(cells, cots, kern, conv_bias.reshape(1, D), norm_gain.reshape(1, D))
 

time: 60.2 us -> 50.8 us (0.84)
  the two profiles are of different devices: /device:TPU:1 before, /device:TPU:81 now
where the time goes in v2:
time: 50.8 us; the launch traced here: 50.6 us
  Pallas kernels  49.3 us (97%)
  local copies, waits for them, and re-layouts  1.3 us (3%)
    pallas_call x1, Pallas kernels, local(): pl.pallas_call(kernel, out_shape=jax.ShapeDtypeStruct((13, 12), F32), in_...  49.3 us
    unnamed x1, local copies, waits for them, and re-layouts  1.3 us

profile of v2, /device:TPU:81, one launch (start us, length us, event | category | flops | bytes accessed | tf_op | source)
XLA Modules:
  0.0 50.6 jit_solution(16189079480135862365)
XLA Ops:
  0.0 49.3 %shard_map.55 = f32[13,12]{1,0:T(8,128)} custom-call(bf16[9,16,3072]{2,1,0:T(8,128)(2,1)} %bitcast.8, bf16[9,16,3072]{2,1,0:T(8,128)(2,1)} %bitcast.9, f32[49,3072]{1,0:T(8,128)} %k_hbm.1, f32[1,3072]{1,0:T(1,128)} %bitcast.10, f32[1,3072]{1,0:T(1,128)} %bitcast.11), custom_call_target="tpu_custom_call" | custom-call | tf_op jit(solution)/shard_map/pallas_call | solution.py:446
  49.3 1.3 %copy.7 = f32[13,12]{1,0:T(8,128)} copy(f32[13,12]{1,0:T(8,128)} %shard_map.55) | data formatting | bytes 1248

commit v3 on v2

--- a/solution.py
+++ b/solution.py
@@ -16,8 +16,9 @@
 TILES = D // LANE
 CHUNK = D // NY
 CT = CHUNK // LANE
-PIECES = 4
+PIECES = 8
 PIECE = D // PIECES
+BATCH = 1
 TAP0 = 8
 TAPN = 40
 START = (0, 6, 14, 22)
@@ -70,9 +71,9 @@
 def kernel(
     x_hbm, u_hbm, k_hbm, b_hbm, g_hbm, out_ref,
     xv, uv, kv, bv, gv, dv, stat,
-    own, half, summed, plane, acc, line, both, part, parts_in, gram, rows, ruler,
-    x_sem, u_sem, k_sem, half_s, half_r, plane_s, plane_r, line_s, line_r,
-    parts_s, parts_r, total_s, total_r, rows_s, rows_r,
+    own, half, summed, plane, acc, line, both, part, parts_in, gram, rows, one, apart, mixed, ready, ruler,
+    x_sem, u_sem, k_sem, tap_sem, half_s, half_r, plane_s, plane_r, line_s, line_r,
+    parts_s, parts_r, total_s, total_r, rows_s, rows_r, one_s, one_r,
 ):
     me_x = lax.axis_index("grp")
     dp = lax.axis_index("dp")
@@ -90,9 +91,8 @@
         pltpu.make_async_copy(ref, ref, sem).wait()
 
     k_copies = [
-        pltpu.make_async_copy(k_hbm.at[pl.ds(TAP0, TAPN)], kv, k_sem.at[0]),
-        pltpu.make_async_copy(b_hbm, bv, k_sem.at[1]),
-        pltpu.make_async_copy(g_hbm, gv, k_sem.at[2]),
+        pltpu.make_async_copy(b_hbm, bv, k_sem.at[0]),
+        pltpu.make_async_copy(g_hbm, gv, k_sem.at[1]),
     ]
     x_copies = [
         pltpu.make_async_copy(
@@ -100,12 +100,18 @@
         )
         for i in range(PIECES)
     ]
+    tap_copies = [
+        pltpu.make_async_copy(
+            k_hbm.at[pl.ds(TAP0, TAPN), pl.ds(i * PIECE, PIECE)], kv.at[:, pl.ds(i * PIECE, PIECE)], tap_sem.at[i]
+        )
+        for i in range(PIECES)
+    ]
     u_copy = pltpu.make_async_copy(u_hbm, uv, u_sem)
     k_copies[0].start()
+    for i in range(PIECES):
+        tap_copies[i].start()
+        x_copies[i].start()
     k_copies[1].start()
-    for copy in x_copies:
-        copy.start()
-    k_copies[2].start()
     u_copy.start()
 
     def turn(v, n, size):
@@ -129,9 +135,11 @@
             tell(me_x, me_y, z, me_c)
 
     k_copies[0].wait()
-    k_copies[1].wait()
+
+    zero = jnp.zeros((CROPS, LANE), F32)
 
     def conv_tile(k, carry):
+        carry = list(carry)
         lanes = pl.ds(pl.multiple_of(k * LANE, LANE), LANE)
         cells = [xv[q, :, lanes].astype(F32) for q in range(CELLS)]
         taps = {}
@@ -146,31 +154,31 @@
                 term = taps[q // 3 - p // 3, q % 3 - p % 3] * cells[q]
                 total = term + bias if total is None else total + term
             dv[p, :, lanes] = total
+            carry[p] = carry[p] + total
+        return tuple(carry)
+
+    def conv_tiles(k, carry):
+        for n in range(3):
+            carry = conv_tile(k * 3 + n, carry)
         return carry
 
+    sums = (zero,) * CELLS
     for i in range(PIECES):
+        tap_copies[i].wait()
         x_copies[i].wait()
-        lax.fori_loop(i * TILES // PIECES, (i + 1) * TILES // PIECES, conv_tile, 0)
-
-    def sum_tile(k, sums):
-        sums = list(sums)
-        for n in range(4):
-            lanes = pl.ds(pl.multiple_of((k * 4 + n) * LANE, LANE), LANE)
-            for p in range(CELLS):
-                sums[p] = sums[p] + dv[p, :, lanes]
-        return tuple(sums)
-
-    zero = jnp.zeros((CROPS, LANE), F32)
-    sums = lax.fori_loop(0, TILES // 4, sum_tile, (zero,) * CELLS)
+        per = TILES // PIECES // 3
+        sums = lax.fori_loop(i * per, (i + 1) * per, conv_tiles, sums)
+
     means = [jnp.sum(s, 1, keepdims=True) * (1.0 / D) for s in sums]
-    k_copies[2].wait()
+    k_copies[1].wait()
     u_copy.wait()
+    all_sums = []
     for first in range(0, CELLS, 3):
 
         def stat_tile(k, sums, first=first):
             sums = list(sums)
-            for n in range(4):
-                lanes = pl.ds(pl.multiple_of((k * 4 + n) * LANE, LANE), LANE)
+            for n in range(8):
+                lanes = pl.ds(pl.multiple_of((k * 8 + n) * LANE, LANE), LANE)
                 gain = gv[:, lanes]
                 for i in range(3):
                     p = first + i
@@ -182,9 +190,10 @@
                     sums[3 * i + 2] = sums[3 * i + 2] + s * d
             return tuple(sums)
 
-        sums = lax.fori_loop(0, TILES // 4, stat_tile, (zero,) * 9)
+        all_sums += lax.fori_loop(0, TILES // 8, stat_tile, (zero,) * 9)
+    for first in range(0, CELLS, 3):
         for i in range(3):
-            var, mean_s, mean_sd = [jnp.sum(s, 1, keepdims=True) * (1.0 / D) for s in sums[3 * i : 3 * i + 3]]
+            var, mean_s, mean_sd = [jnp.sum(s, 1, keepdims=True) * (1.0 / D) for s in all_sums[3 * (first + i) : 3 * (first + i) + 3]]
             scale = lax.rsqrt(var + 1e-06)
             stat[0, first + i] = jnp.broadcast_to(scale, (CROPS, LANE))
             stat[1, first + i] = jnp.broadcast_to(scale * mean_s, (CROPS, LANE))
@@ -192,7 +201,7 @@
 
     sub = lax.broadcasted_iota(jnp.int32, (8, LANE), 0)
 
-    def grad_tile(y, t):
+    def grad_tile(i, y, t):
         lanes = pl.ds(pl.multiple_of(y * CHUNK + t * LANE, LANE), LANE)
         gain = gv[:, lanes]
         grads = []
@@ -201,19 +210,20 @@
             d = dv[p, :, lanes]
             u = uv[p, :, lanes].astype(F32)
             scale = stat[0, p]
-            grad = u * gain * scale - stat[1, p] - d * stat[2, p]
-            ud = u * (d * scale)
+            u_scaled = u * scale
+            grad = u_scaled * gain - (stat[1, p] + d * stat[2, p])
+            ud = u_scaled * d
             grads.append(grad)
             sum_g = grad if p == 0 else sum_g + grad
             sum_ud = ud if p == 0 else sum_ud + ud
             sum_u = u if p == 0 else sum_u + u
         cells = [xv[q, :, lanes].astype(F32) for q in range(CELLS)]
         parts = []
-        for i in range(-2, 3):
+        for di in range(-2, 3):
             for j in range(-2, 3):
                 total = None
                 for p in range(CELLS):
-                    a, b = p // 3 + i, p % 3 + j
+                    a, b = p // 3 + di, p % 3 + j
                     if 0 <= a < 3 and 0 <= b < 3:
                         term = grads[p] * cells[3 * a + b]
                         total = term if total is None else total + term
@@ -227,53 +237,61 @@
                 group += parts[START[x] + c * COUNT[x] : START[x] + (c + 1) * COUNT[x]] + [none] * (4 - COUNT[x])
             for h in range(2):
                 packed = pack_rows(group[8 * h : 8 * h + 8], sub)
-                own[y, c, 2 * h, t] = packed[:4]
-                own[y, c, 2 * h + 1, t] = packed[4:]
+                own[i, c, 2 * h, t] = packed[:4]
+                own[i, c, 2 * h + 1, t] = packed[4:]
 
     def chunk_of(i):
-        off = jnp.where(i % 2 == 0, 4 + i // 2, 4 - (i + 1) // 2)
-        return (me_y + off) % NY
-
-    def half_copy(i):
+        return (me_y + jnp.where(i % 2 == 0, 4 + i // 2, 4 - (i + 1) // 2)) % NY
+
+    def half_copy(k):
+        span = pl.ds(BATCH * k, BATCH)
         return remote(
-            own.at[chunk_of(i), 1 - me_c], half.at[i], half_s.at[i], half_r.at[i], me_x, me_y, me_z, 1 - me_c
+            own.at[span, 1 - me_c], half.at[span], half_s.at[k], half_r.at[k], me_x, me_y, me_z, 1 - me_c
         )
 
     me_slot = me_x * NY + me_y
 
     def add_half(i):
-        half_copy(i).wait_recv()
-        y = chunk_of(i)
         for x in range(NX):
             for t in range(CT):
-                summed[i, x, t] = own[y, me_c, x, t] + half[i, x, t]
+                summed[i, x, t] = own[i, me_c, x, t] + half[i, x, t]
 
     def plane_copy(i, x):
         return remote(
             summed.at[i, x], plane.at[me_slot], plane_s, plane_r, x, chunk_of(i), me_z, me_c
         )
 
+    def pass_on(i):
+        add_half(i)
+        for n in (2, 1, 3):
+            plane_copy(i, near_x[n]).start()
+
     pl.semaphore_wait(barrier, NX * NY + jnp.where(hub, 0, 1))
 
-    @pl.loop(0, NY)
-    def _(i):
-        y = chunk_of(i)
-
-        @pl.loop(0, CT)
-        def _(t):
-            grad_tile(y, t)
-
-        half_copy(i).start()
-
-        @pl.when(i > 0)
+    @pl.loop(0, NY // BATCH)
+    def _(k):
+        @pl.loop(0, BATCH)
+        def _(n):
+            i = BATCH * k + n
+            y = chunk_of(i)
+            for t in range(CT):
+                grad_tile(i, y, t)
+
+        half_copy(k).start()
+
+        @pl.when(k > 0)
         def _():
-            add_half(i - 1)
-            for n in (2, 1, 3, 0):
-                plane_copy(i - 1, near_x[n]).start()
-
-    add_half(NY - 1)
-    for n in (2, 1, 3):
-        plane_copy(NY - 1, near_x[n]).start()
+            half_copy(k - 1).wait_recv()
+            for n in range(BATCH):
+                i = BATCH * (k - 1) + n
+                pass_on(i)
+                plane_copy(i, me_x).start()
+
+    half_copy(NY // BATCH - 1).wait_recv()
+    for i in range(NY - BATCH, NY):
+        pass_on(i)
+        if i < NY - 1:
+            plane_copy(i, me_x).start()
     for t in range(CT):
         plane[me_slot, t] = summed[NY - 1, me_x, t]
 
@@ -297,15 +315,21 @@
     row4 = lax.broadcasted_iota(jnp.int32, (4, LANE), 0)
     lane4 = lax.broadcasted_iota(jnp.int32, (4, LANE), 1)
 
-    def row_copy(t, place, x, e):
+    soon = me_z < NZ // 2
+    feeds_soon = me_y < NY // 2
+
+    def row_copy(src, dst, send, recv, x, e):
         return pltpu.make_async_remote_copy(
-            src_ref=both.at[t], dst_ref=rows.at[place], send_sem=rows_s, recv_sem=rows_r,
+            src_ref=src, dst_ref=dst, send_sem=send, recv_sem=recv,
             device_id=(x, 2 * NY * NC * me_y + e), device_id_type=MESH,
         )
 
     @pl.when(jnp.logical_not(hub))
     def _():
         line_copy.start()
+
+    @pl.when(soon & jnp.logical_not(hub))
+    def _():
         take(gram, total_r)
 
     @pl.when(hub)
@@ -338,74 +362,115 @@
             ).start()
         parts_in[slot] = part[...]
 
-        for e in range(2 * NY * NC):
-            for n, t in enumerate(TILES_OF[e]):
-                if e < NC:
-                    here = (me_y == 0) & (me_c == e)
-
-                    @pl.when(here)
-                    def _(t=t, n=n):
-                        pltpu.make_async_copy(both.at[t], rows.at[2 * me_c + n], rows_r).start()
-
-                    @pl.when(jnp.logical_not(here))
-                    def _(t=t, n=n, e=e):
-                        row_copy(t, 2 * me_c + n, me_x, e).start()
-                else:
-                    row_copy(t, 2 * me_c + n, me_x, e).start()
-
-        @pl.when(odd)
+        @pl.when(feeds_soon)
         def _():
             for e in range(2 * NY * NC):
                 for n, t in enumerate(TILES_OF[e]):
-                    row_copy(t, 4 + n, odd_x, e).start()
+                    copy = row_copy(both.at[t], rows.at[2 * me_c + n], rows_s, rows_r, me_x, e)
+                    if e < NC:
+                        here = (me_y == 0) & (me_c == e)
+
+                        @pl.when(here)
+                        def _(t=t, n=n):
+                            pltpu.make_async_copy(both.at[t], rows.at[2 * me_c + n], rows_r).start()
+
+                        pl.when(jnp.logical_not(here))(copy.start)
+                    else:
+                        copy.start()
+
+        @pl.when(feeds_soon & odd)
+        def _():
+            for t in range(CT):
+                for g in range(NX):
+                    v = sums[t][g]
+                    apart[t, g : g + 1] = jnp.where(odd_low, v[2:3], v[0:1])
+            for e in range(2 * NY * NC):
+                for n, t in enumerate(TILES_OF[e]):
+                    row_copy(apart.at[t], one.at[n], one_s, one_r, odd_x, e).start()
 
         take(parts_in.at[pl.ds(0, NX * NY * NC - 1)], parts_r)
         totals = [parts_in[n] for n in range(4)]
         for n in range(4, NX * NY * NC):
             totals[n % 4] = totals[n % 4] + parts_in[n]
         gram[...] = (totals[0] + totals[1]) + (totals[2] + totals[3])
-        for z in range(1, NZ):
+        for z in range(1, NZ // 2):
             total_copy(z).start()
-
-    total = gram[...]
-
-    def entry(k):
-        return total if k == 0 else pltpu.roll(total, LANE - k, 1)
-
-    n0, p01, p02, p03, n1, p12, p13, n2, p23, n3 = [entry(k) for k in (0, 1, 2, 3, 5, 6, 7, 10, 11, 15)]
-    a0 = 1.0 - p01 / (2.0 * n0)
-    a1 = 1.0 - p01 / (2.0 * n1)
-    a2 = 1.0 - p23 / (2.0 * n2)
-    a3 = 1.0 - p23 / (2.0 * n3)
-    inner = a0 * (a2 * p02 + a3 * p03) + a1 * (a2 * p12 + a3 * p13)
-    low = a0 * (a0 * n0 + a1 * p01) + a1 * (a0 * p01 + a1 * n1)
-    high = a2 * (a2 * n2 + a3 * p23) + a3 * (a2 * p23 + a3 * n3)
-    lo = 1.0 - inner / (2.0 * low)
-    hi = 1.0 - inner / (2.0 * high)
-    coeffs = [lo * a0, lo * a1, hi * a2, hi * a3]
-    layer = jnp.where(me_x == NX - 1, row4 + 1, 0)
-    first_layer = [jnp.sum(jnp.where(lane4 == 0, c, 0.0), 1, keepdims=True) for c in coeffs]
-    row_layer = [jnp.sum(jnp.where(lane4 == 16 * layer, c, 0.0), 1, keepdims=True) for c in coeffs]
 
     place = me_z % 2 * 16 + me_y * 2 + me_c
     lanes_off = 12 * place % LANE
     straddles = lanes_off + 12 > LANE
     inside = (me_x == 1) | (me_x == NX - 2)
-    for is_inside in (False, True):
+
+    def blend_here():
+        total = gram[...]
+
+        def entry(k):
+            return total if k == 0 else pltpu.roll(total, LANE - k, 1)
+
+        n0, p01, p02, p03, n1, p12, p13, n2, p23, n3 = [entry(k) for k in (0, 1, 2, 3, 5, 6, 7, 10, 11, 15)]
+        a0 = 1.0 - p01 / (2.0 * n0)
+        a1 = 1.0 - p01 / (2.0 * n1)
+        a2 = 1.0 - p23 / (2.0 * n2)
+        a3 = 1.0 - p23 / (2.0 * n3)
+        inner = a0 * (a2 * p02 + a3 * p03) + a1 * (a2 * p12 + a3 * p13)
+        low = a0 * (a0 * n0 + a1 * p01) + a1 * (a0 * p01 + a1 * n1)
+        high = a2 * (a2 * n2 + a3 * p23) + a3 * (a2 * p23 + a3 * n3)
+        lo = 1.0 - inner / (2.0 * low)
+        hi = 1.0 - inner / (2.0 * high)
+        coeffs = [lo * a0, lo * a1, hi * a2, hi * a3]
+        layer = jnp.where(me_x == NX - 1, row4 + 1, 0)
+        first_layer = [jnp.sum(jnp.where(lane4 == 0, c, 0.0), 1, keepdims=True) for c in coeffs]
+        row_layer = [jnp.sum(jnp.where(lane4 == 16 * layer, c, 0.0), 1, keepdims=True) for c in coeffs]
+
+        @pl.when(hub & jnp.logical_not(feeds_soon))
+        def _():
+            mine = [jnp.where(me_c == 1, r, f) for r, f in zip(row_layer, first_layer)]
+            for t in range(CT):
+                mixed[t] = sum(both[t, g] * mine[g] for g in range(NX))
+            for e in range(2 * NY * NC):
+                for n, t in enumerate(TILES_OF[e]):
+                    row_copy(mixed.at[t], ready.at[2 * me_c + n], rows_s, rows_r, me_x, e).start()
+
+            @pl.when(odd)
+            def _():
+                for e in range(2 * NY * NC):
+                    for n, t in enumerate(TILES_OF[e]):
+                        row_copy(mixed.at[t], ready.at[4 + n], rows_s, rows_r, odd_x, e).start()
+
         for is_two in (False, True):
 
-            @pl.when((inside == is_inside) & (straddles == is_two))
-            def _(count=(2 + is_inside) * (1 + is_two)):
-                take(rows.at[pl.ds(0, count)], rows_r)
+            @pl.when(straddles == is_two)
+            def _(count=1 + is_two):
+                take(rows.at[pl.ds(0, 2 * count)], rows_r)
+
+                @pl.when(inside)
+                def _():
+                    take(one.at[pl.ds(0, count)], one_r)
+
+        for n in range(2):
+            for k, coeff in enumerate((first_layer, row_layer)):
+                ready[2 * k + n] = sum(rows[2 * k + n, g] * coeff[g] for g in range(NX))
+            single = sum(one[n, g : g + 1] * first_layer[g][:1] for g in range(NX))
+            ready[4 + n] = jnp.broadcast_to(single, (4, LANE))
+
+    @pl.when(soon)
+    def _():
+        blend_here()
+
+    @pl.when(jnp.logical_not(soon))
+    def _():
+        for is_inside in (False, True):
+            for is_two in (False, True):
+
+                @pl.when((inside == is_inside) & (straddles == is_two))
+                def _(count=(2 + is_inside) * (1 + is_two)):
+                    take(ready.at[pl.ds(0, count)], rows_r)
 
     shift = (LANE - lanes_off) % LANE
     keep = lane4 + lanes_off < LANE
     blended = []
-    for k, coeff in enumerate((first_layer, row_layer, first_layer)):
-        by_tile = []
-        for n in range(2):
-            value = sum(rows[2 * k + n, g] * coeff[g] for g in range(NX))
-            by_tile.append(pltpu.roll(value, shift, 1))
+    for k in range(3):
+        by_tile = [pltpu.roll(ready[2 * k + n], shift, 1) for n in range(2)]
         blended.append(jnp.where(keep, by_tile[0], by_tile[1])[:, :12])
     out_ref[...] = jnp.zeros_like(out_ref)
     for x in range(NX):
@@ -415,9 +480,10 @@
             for at, k, j in OUT_ROWS[x]:
                 out_ref[at : at + 1] = blended[k][j : j + 1]
 
-    @pl.loop(0, NY)
-    def _(i):
-        half_copy(i).wait_send()
+
+    @pl.loop(0, NY // BATCH)
+    def _(k):
+        half_copy(k).wait_send()
 
     take(plane.at[pl.ds(0, NX * NY - 1)], plane_s)
 
@@ -428,13 +494,22 @@
     @pl.when(hub)
     def _():
         take(parts_in.at[pl.ds(0, NX * NY * NC - 1)], parts_s)
-        take(parts_in.at[pl.ds(0, NZ - 1)], total_s)
+        take(parts_in.at[pl.ds(0, NZ // 2 - 1)], total_s)
+        for is_first in (False, True):
+
+            @pl.when(feeds_soon & ((me_y == 0) == is_first))
+            def _(count=4 * (SENDS - is_first)):
+                take(ruler.at[pl.ds(0, count)], rows_s)
+
+        @pl.when(feeds_soon & odd)
+        def _():
+            take(ruler.at[pl.ds(0, SENDS)], one_s)
+
         for is_odd in (False, True):
-            for is_first in (False, True):
-
-                @pl.when((odd == is_odd) & ((me_y == 0) == is_first))
-                def _(count=SENDS * (1 + is_odd) - is_first):
-                    take(ruler.at[pl.ds(0, count)], rows_s)
+
+            @pl.when(jnp.logical_not(feeds_soon) & (odd == is_odd))
+            def _(count=SENDS * (1 + is_odd)):
+                take(ruler.at[pl.ds(0, count)], rows_s)
 
 
 def local(crops_in, cotangent, kern, conv_bias, norm_gain):
@@ -466,14 +541,19 @@
             vmem((1, LANE), F32),
             vmem((NX * NY * NC, 1, LANE), F32),
             vmem((1, LANE), F32),
-            vmem((6, NX, 4, LANE), F32),
-            vmem((2 * SENDS, NX, 4, LANE), F32),
+            vmem((4, NX, 4, LANE), F32),
+            vmem((2, NX, LANE), F32),
+            vmem((CT, NX, LANE), F32),
+            vmem((CT, 4, LANE), F32),
+            vmem((6, 4, LANE), F32),
+            vmem((4 * SENDS, 4, LANE), F32),
             dma((PIECES,)),
             dma,
-            dma((3,)),
-            dma((NY,)),
-            dma((NY,)),
-            dma, dma, dma, dma, dma, dma, dma, dma, dma, dma,
+            dma((2,)),
+            dma((PIECES,)),
+            dma((NY // BATCH,)),
+            dma((NY // BATCH,)),
+            dma, dma, dma, dma, dma, dma, dma, dma, dma, dma, dma, dma,
         ],
         compiler_params=pltpu.CompilerParams(
             collective_id=0, has_side_effects=True, vmem_limit_bytes=61 * 1024 * 1024

time: 50.8 us -> 48.7 us (0.959)
  the two profiles are of different devices: /device:TPU:81 before, /device:TPU:1 now
where the time goes in v3:
time: 48.7 us; the launch traced here: 48.5 us
  Pallas kernels  47.2 us (97%)
  local copies, waits for them, and re-layouts  1.3 us (3%)
    pallas_call x1, Pallas kernels, local(): pl.pallas_call(kernel, out_shape=jax.ShapeDtypeStruct((13, 12), F32), in_...  47.2 us
    unnamed x1, local copies, waits for them, and re-layouts  1.3 us

profile of v3, /device:TPU:1, one launch (start us, length us, event | category | flops | bytes accessed | tf_op | source)
XLA Modules:
  0.0 48.5 jit_solution(2484434522815133109)
XLA Ops:
  0.0 47.2 %shard_map.55 = f32[13,12]{1,0:T(8,128)} custom-call(bf16[9,16,3072]{2,1,0:T(8,128)(2,1)} %bitcast.8, bf16[9,16,3072]{2,1,0:T(8,128)(2,1)} %bitcast.9, f32[49,3072]{1,0:T(8,128)} %k_hbm.1, f32[1,3072]{1,0:T(1,128)} %bitcast.10, f32[1,3072]{1,0:T(1,128)} %bitcast.11), custom_call_target="tpu_custom_call" | custom-call | tf_op jit(solution)/shard_map/pallas_call | solution.py:521
  47.2 1.3 %copy.7 = f32[13,12]{1,0:T(8,128)} copy(f32[13,12]{1,0:T(8,128)} %shard_map.55) | data formatting | bytes 1248

commit v4 on v3

--- a/solution.py
+++ b/solution.py
@@ -18,6 +18,7 @@
 CT = CHUNK // LANE
 PIECES = 8
 PIECE = D // PIECES
+BEHIND = 3
 BATCH = 1
 TAP0 = 8
 TAPN = 40
@@ -113,6 +114,8 @@
         x_copies[i].start()
     k_copies[1].start()
     u_copy.start()
+
+    plane[...] = jnp.zeros_like(plane)
 
     def turn(v, n, size):
         return v if n == 0 else jnp.where(v + n >= size, v + n - size, v + n)
@@ -257,14 +260,25 @@
                 summed[i, x, t] = own[i, me_c, x, t] + half[i, x, t]
 
     def plane_copy(i, x):
+        use = pl.ds(0, COUNT[x])
         return remote(
-            summed.at[i, x], plane.at[me_slot], plane_s, plane_r, x, chunk_of(i), me_z, me_c
+            summed.at[i, x, :, use], plane.at[me_slot, :, use], plane_s, plane_r, x, chunk_of(i), me_z, me_c
         )
 
     def pass_on(i):
         add_half(i)
-        for n in (2, 1, 3):
-            plane_copy(i, near_x[n]).start()
+        for x in range(NX):
+
+            @pl.when(me_x != x)
+            def _(x=x):
+                plane_copy(i, x).start()
+
+    def pass_own_x(i):
+        for x in range(NX):
+
+            @pl.when(me_x == x)
+            def _(x=x):
+                plane_copy(i, x).start()
 
     pl.semaphore_wait(barrier, NX * NY + jnp.where(hub, 0, 1))
 
@@ -279,23 +293,30 @@
 
         half_copy(k).start()
 
-        @pl.when(k > 0)
+        @pl.when(k >= BEHIND)
         def _():
-            half_copy(k - 1).wait_recv()
+            half_copy(k - BEHIND).wait_recv()
             for n in range(BATCH):
-                i = BATCH * (k - 1) + n
+                i = BATCH * (k - BEHIND) + n
                 pass_on(i)
-                plane_copy(i, me_x).start()
-
-    half_copy(NY // BATCH - 1).wait_recv()
-    for i in range(NY - BATCH, NY):
+                pass_own_x(i)
+
+    for i in range(NY - BEHIND * BATCH, NY):
+        if i % BATCH == 0:
+            half_copy(i // BATCH).wait_recv()
         pass_on(i)
         if i < NY - 1:
-            plane_copy(i, me_x).start()
+            pass_own_x(i)
     for t in range(CT):
         plane[me_slot, t] = summed[NY - 1, me_x, t]
 
-    take(plane.at[pl.ds(0, NX * NY - 1)], plane_r)
+    short = (me_x == 0) | (me_x == NX - 1)
+    for is_short in (False, True):
+
+        @pl.when(short == is_short)
+        def _(use=pl.ds(0, 4 - is_short)):
+            take(plane.at[pl.ds(0, NX * NY - 1), :, use], plane_r)
+
     for g in range(NX):
         for t in range(CT):
             total = plane[g * NY, t]
@@ -485,7 +506,13 @@
     def _(k):
         half_copy(k).wait_send()
 
-    take(plane.at[pl.ds(0, NX * NY - 1)], plane_s)
+    for is_short in (False, True):
+
+        @pl.when(short == is_short)
+        def _(one_more=is_short):
+            take(plane.at[pl.ds(0, NX * NY // 2 - 1 + one_more)], plane_s)
+            take(plane.at[pl.ds(0, NX * NY // 2 - one_more), :, pl.ds(0, 3)], plane_s)
+
 
     @pl.when(jnp.logical_not(hub))
     def _():

time: 48.7 us -> 48.6 us (level)
  no operation moved by 1% of the time
where the time goes in v4:
time: 48.6 us; the launch traced here: 48.4 us
  Pallas kernels  47.1 us (97%)
  local copies, waits for them, and re-layouts  1.3 us (3%)
    pallas_call x1, Pallas kernels, local(): pl.pallas_call(kernel, out_shape=jax.ShapeDtypeStruct((13, 12), F32), in_...  47.1 us
    unnamed x1, local copies, waits for them, and re-layouts  1.3 us

profile of v4, /device:TPU:1, one launch (start us, length us, event | category | flops | bytes accessed | tf_op | source)
XLA Modules:
  0.0 48.4 jit_solution(6604173889420369627)
XLA Ops:
  0.0 47.1 %shard_map.55 = f32[13,12]{1,0:T(8,128)} custom-call(bf16[9,16,3072]{2,1,0:T(8,128)(2,1)} %bitcast.8, bf16[9,16,3072]{2,1,0:T(8,128)(2,1)} %bitcast.9, f32[49,3072]{1,0:T(8,128)} %k_hbm.1, f32[1,3072]{1,0:T(1,128)} %bitcast.10, f32[1,3072]{1,0:T(1,128)} %bitcast.11), custom_call_target="tpu_custom_call" | custom-call | tf_op jit(solution)/shard_map/pallas_call | solution.py:548
  47.1 1.3 %copy.7 = f32[13,12]{1,0:T(8,128)} copy(f32[13,12]{1,0:T(8,128)} %shard_map.55) | data formatting | bytes 1248

commit v5 on v4

--- a/solution.py
+++ b/solution.py
@@ -116,6 +116,7 @@
     u_copy.start()
 
     plane[...] = jnp.zeros_like(plane)
+    line[...] = jnp.zeros_like(line)
 
     def turn(v, n, size):
         return v if n == 0 else jnp.where(v + n >= size, v + n - size, v + n)
@@ -324,7 +325,16 @@
                 total = total + plane[g * NY + y, t]
             acc[t, g] = total
 
-    line_copy = remote(acc, line.at[me_z], line_s, line_r, me_x, me_y, 0, me_c)
+    def line_copy(use):
+        return remote(acc.at[:, :, use], line.at[me_z, :, :, use], line_s, line_r, me_x, me_y, 0, me_c)
+
+    def by_rows(fn):
+        for is_short in (False, True):
+
+            @pl.when(short == is_short)
+            def _(use=pl.ds(0, 4 - is_short)):
+                fn(use)
+
 
     def total_copy(z):
         return remote(gram, gram, total_s, total_r, me_x, me_y, z, me_c)
@@ -347,7 +357,7 @@
 
     @pl.when(jnp.logical_not(hub))
     def _():
-        line_copy.start()
+        by_rows(lambda use: line_copy(use).start())
 
     @pl.when(soon & jnp.logical_not(hub))
     def _():
@@ -355,7 +365,7 @@
 
     @pl.when(hub)
     def _():
-        take(line.at[pl.ds(1, NZ - 1)], line_r)
+        by_rows(lambda use: take(line.at[pl.ds(1, NZ - 1), :, :, use], line_r))
         sums = []
         for t in range(CT):
             of_tile = []
@@ -516,7 +526,7 @@
 
     @pl.when(jnp.logical_not(hub))
     def _():
-        line_copy.wait_send()
+        by_rows(lambda use: line_copy(use).wait_send())
 
     @pl.when(hub)
     def _():

time: 48.6 us -> 48.6 us (level)
  no operation moved by 1% of the time
where the time goes in v5:
time: 48.6 us; the launch traced here: 48.4 us
  Pallas kernels  47.1 us (97%)
  local copies, waits for them, and re-layouts  1.3 us (3%)
    pallas_call x1, Pallas kernels, local(): pl.pallas_call(kernel, out_shape=jax.ShapeDtypeStruct((13, 12), F32), in_...  47.1 us
    unnamed x1, local copies, waits for them, and re-layouts  1.3 us

profile of v5, /device:TPU:1, one launch (start us, length us, event | category | flops | bytes accessed | tf_op | source)
XLA Modules:
  0.0 48.4 jit_solution(17772533768624259305)
XLA Ops:
  0.0 47.1 %shard_map.55 = f32[13,12]{1,0:T(8,128)} custom-call(bf16[9,16,3072]{2,1,0:T(8,128)(2,1)} %bitcast.8, bf16[9,16,3072]{2,1,0:T(8,128)(2,1)} %bitcast.9, f32[49,3072]{1,0:T(8,128)} %k_hbm.1, f32[1,3072]{1,0:T(1,128)} %bitcast.10, f32[1,3072]{1,0:T(1,128)} %bitcast.11), custom_call_target="tpu_custom_call" | custom-call | tf_op jit(solution)/shard_map/pallas_call | solution.py:558
  47.1 1.3 %copy.7 = f32[13,12]{1,0:T(8,128)} copy(f32[13,12]{1,0:T(8,128)} %shard_map.55) | data formatting | bytes 1248
